TPU v7x, 32 devices: a whole 2x2x4 slice. The times are simulated.
32 devices in a mesh: grp: 4 (over y, x), tile: 8 (over z, core).
Axes of the slice: x: 2, y: 2, z: 4, core: 2. Of those that a mesh axis runs over, the one named last changes fastest.
Arguments:
- adjoint_in: float32 [32768, 128], P(('grp', 'tile')), may hold values from -6 to 6
- departure: int32 [2, 32768], P(None, ('grp', 'tile')), may hold values from 0 to 32767, as said below
- fraction: float32 [2, 32768], P(None, ('grp', 'tile')), may hold values from 0 to 1
- level_map: float32 [2, 128, 128], replicated, may hold values from -0.5 to 0.5
- coarse_map: float32 [128, 4, 4], replicated, may hold values from -3 to 3
Outputs:
- adjoint_out: float32 [32768, 128], P(('grp', 'tile'))
Inputs may be any that keep to these rules, and one draw needn't show every extreme that they name: For each step, the departure cell of a column lies in the same block row, on the device whose tile index differs from the column's own by at most 2, counted periodically along tile. Of the columns of one device, at most 512 have departure cells on any one device, and on every device exactly 512 of them share one device.
All inputs are finite; a program needn't handle non-finite values.
Results may differ from a plain program's by a relative error of at most 0.00013.
Values sent between devices are 32-bit elements; how exact they have to be, the bound alone decides.
A program may use at most 64 MiB of HBM per device.

v0:
```python
import functools

import jax
import jax.numpy as jnp
from jax import lax
from jax.experimental import pallas as pl
from jax.experimental.pallas import tpu as pltpu
from jax.sharding import PartitionSpec as P

REACH = 2
SHIFTS = (2, -2, 1, -1, 0)
REMOTE = 4
BF16 = jnp.bfloat16
F32 = jnp.float32


def cubic_weights(a):
    return [
        -a * (1.0 - a) * (2.0 - a) / 6.0,
        (1.0 + a) * (1.0 - a) * (2.0 - a) / 2.0,
        (1.0 + a) * a * (2.0 - a) / 2.0,
        -(1.0 + a) * a * (1.0 - a) / 6.0,
    ]


def split(x):
    high = x.astype(BF16)
    return high, (x - high.astype(F32)).astype(BF16)


def dot(a, b):
    return jnp.dot(a, b, preferred_element_type=F32)


def dot_nt(a, b):
    return lax.dot_general(a, b, (((1,), (1,)), ((), ())), preferred_element_type=F32)


def kernel(
    n_grp, n_tile, x_ref, meta_ref, lm_ref, cm_ref, out_ref,
    tri, slots, pick, lifted, rows_out, rows_in, meta_out, meta_in, rows_hl,
    land, edge, edge_in, field, grp_in, grp_mid, grp_last,
    rows_ss, rows_rs, meta_ss, meta_rs, edge_ss, edge_rs, grp_ss, grp_rs,
):
    cols = x_ref.shape[0]
    lev = x_ref.shape[1]
    half = cols // 2
    grp = lax.axis_index("grp")
    tile = lax.axis_index("tile")

    def at_tile(by):
        return {"tile": lax.rem(tile + (by + n_tile), n_tile)}

    def at_grp(g):
        return {"grp": g}

    barrier = pltpu.get_barrier_semaphore()
    for by in SHIFTS[:REMOTE]:
        pl.semaphore_signal(barrier, inc=1, device_id=at_tile(by), device_id_type=pl.DeviceIdType.MESH)
    for step in range(1, n_grp):
        pl.semaphore_signal(
            barrier, inc=1, device_id=at_grp(lax.rem(grp + step, n_grp)),
            device_id_type=pl.DeviceIdType.MESH,
        )
    pl.semaphore_wait(barrier, REMOTE + n_grp - 1)

    sent = []
    metas = ([], [])

    def send(src, dst, ss, rs, where):
        copy = pltpu.make_async_remote_copy(
            src_ref=src, dst_ref=dst, send_sem=ss, recv_sem=rs,
            device_id=where, device_id_type=pl.DeviceIdType.MESH,
        )
        copy.start()
        sent.append(copy)
        return copy

    block = 128

    @pl.loop(0, cols // block)
    def _(i):
        r = lax.broadcasted_iota(jnp.int32, (block, cols), 0) + i * block
        c = lax.broadcasted_iota(jnp.int32, (block, cols), 1)
        tri[pl.ds(pl.multiple_of(i * block, block), block), :] = jnp.where(r < c, 1.0, 0.0).astype(BF16)

    row8 = lax.broadcasted_iota(jnp.int32, (8, cols), 0)
    wanted = jnp.full((8, cols), -100.0, F32)
    for j, by in enumerate(SHIFTS):
        wanted = jnp.where(row8 == j, float(by), wanted)
    hot = jnp.concatenate([wanted == meta_ref[1, 5:6, :], wanted == meta_ref[0, 5:6, :]], axis=0)
    before = dot(jnp.where(hot, 1.0, 0.0).astype(BF16), tri[...])
    slots[...] = jnp.where(hot, before, -1.0).astype(jnp.int32)

    def build_pick(t, j):
        @pl.loop(0, half // block)
        def _(i):
            r = lax.broadcasted_iota(jnp.int32, (block, cols), 0) + i * block
            hit = r == slots[8 * t + j : 8 * t + j + 1, :]
            pick[t, j, pl.ds(pl.multiple_of(i * block, block), block), :] = jnp.where(hit, 1.0, 0.0).astype(BF16)

    def pack_meta(t, j):
        whole = meta_ref[1 - t]
        a = whole.astype(BF16)
        rest = whole - a.astype(F32)
        b = rest.astype(BF16)
        parts = jnp.concatenate([a.astype(F32), b.astype(F32)], axis=0).astype(BF16)
        got = dot_nt(parts, pick[t, j])
        return got[:8] + got[8:]

    def do_meta(t):
        for j in range(REMOTE):
            meta_out[t, j] = pack_meta(t, j)
            metas[t].append(
                send(meta_out.at[t, j], meta_in.at[t, j], meta_ss.at[t, j], meta_rs.at[t, j], at_tile(SHIFTS[j]))
            )
        meta_in[t, REMOTE] = pack_meta(t, REMOTE)

    def spread(cells, parcel):
        place = parcel[0:1].astype(jnp.int32)
        result = jnp.zeros(cells.shape, F32)
        for k in range(4):
            result = jnp.where(cells == place + (k - 1), parcel[1 + k : 2 + k], result)
        return split(result)

    def product(s_high, s_low):
        wide = dot(s_high, rows_hl[...])
        return wide[:, :lev] + wide[:, lev:] + dot(s_low, rows_hl[:, :lev])

    def edge_part(t, j):
        high, low = split(rows_in[t, j])
        rows_hl[:, :lev] = high
        rows_hl[:, lev:] = low
        r = lax.broadcasted_iota(jnp.int32, (16, half), 0)
        cells = jnp.where(r == 0, -1, jnp.where(r <= 2, cols - 1 + r, -100))
        return product(*spread(cells, meta_in[t, j]))[:8]

    def deposit(t, j, first):
        size = 256

        @pl.loop(0, cols // size)
        def _(i):
            cells = lax.broadcasted_iota(jnp.int32, (size, half), 0) + i * size
            part = product(*spread(cells, meta_in[t, j]))
            at = pl.ds(pl.multiple_of(i * size, size), size)
            if first:
                land[t, at, :] = part
            else:
                land[t, at, :] += part

    def transport(t, src):
        m_high, m_low = split(lm_ref[1 - t])
        f_high, f_low = split(src[...])
        lift = dot_nt(f_high, m_high) + dot_nt(f_low, m_high) + dot_nt(f_high, m_low)
        l_high, l_low = split(lift)
        lifted[:, :lev] = l_high
        lifted[:, lev:] = l_low
        copies = []
        for j in range(REMOTE + 1):
            if t == 0:
                build_pick(t, j)
            both = dot(pick[t, j], lifted[...])
            packed = both[:, :lev] + both[:, lev:]
            if j < REMOTE:
                rows_out[t, j] = packed
                copies.append(
                    send(rows_out.at[t, j], rows_in.at[t, j], rows_ss.at[t, j], rows_rs.at[t, j], at_tile(SHIFTS[j]))
                )
            else:
                rows_in[t, j] = packed
        if t == 0:
            do_meta(0)
        border = edge_part(t, REMOTE)
        deposit(t, REMOTE, True)
        if t == 0:
            for j in range(REMOTE + 1):
                build_pick(1, j)
            do_meta(1)
        for n, j in enumerate((2, 3, 0, 1)):
            copies[j].wait_recv()
            metas[t][j].wait_recv()
            border = border + edge_part(t, j)
            if n == REMOTE - 1:
                edge[t] = border
                to_next = send(edge.at[t], edge_in.at[t, 0], edge_ss.at[t, 0], edge_rs.at[t, 0], at_tile(1))
                to_prev = send(edge.at[t], edge_in.at[t, 1], edge_ss.at[t, 1], edge_rs.at[t, 1], at_tile(-1))
            deposit(t, j, False)
        to_next.wait_recv()
        to_prev.wait_recv()
        r = lax.broadcasted_iota(jnp.int32, (8, lev), 0)
        from_prev = edge_in[t, 0]
        from_next = edge_in[t, 1]
        land[t, 0:8, :] += jnp.where(r == 0, from_prev[1:2], jnp.where(r == 1, from_prev[2:3], 0.0))
        land[t, cols - 8 : cols, :] += jnp.where(r == 7, from_next[0:1], 0.0)

    def coarse(b, e):
        return cm_ref[b, pl.ds(e, 1), :]

    transport(0, x_ref)

    if n_grp == 4:
        flip_x = grp + 1 - 2 * lax.rem(grp, 2)
        flip_y = lax.rem(grp + 2, 4)
        orders = ((flip_x, flip_y), (flip_y, flip_x))
        firsts = []
        lasts = []
        for h, (near, far) in enumerate(orders):
            at = pl.ds(h * half, half)
            firsts.append(send(land.at[0, at], grp_in.at[0, at], grp_ss.at[0, h], grp_rs.at[0, h], at_grp(near)))
        for h, (near, far) in enumerate(orders):
            at = pl.ds(h * half, half)
            firsts[h].wait_recv()
            grp_mid[at, :] = coarse(far, grp) * land[0, at, :] + coarse(far, near) * grp_in[0, at, :]
            lasts.append(send(grp_mid.at[at], grp_last.at[at], grp_ss.at[1, h], grp_rs.at[1, h], at_grp(far)))
        for h, (near, far) in enumerate(orders):
            at = pl.ds(h * half, half)
            field[at, :] = coarse(grp, grp) * land[0, at, :] + coarse(grp, near) * grp_in[0, at, :]
        for h in range(2):
            at = pl.ds(h * half, half)
            lasts[h].wait_recv()
            field[at, :] += grp_last[at, :]
    else:
        copies = []
        for step in range(1, n_grp):
            to = lax.rem(grp + step, n_grp)
            copies.append(
                send(land.at[0], grp_in.at[step - 1], grp_ss.at[step - 1, 0], grp_rs.at[step - 1, 0], at_grp(to))
            )
        field[...] = coarse(grp, grp) * land[0]
        for step in range(1, n_grp):
            copies[step - 1].wait_recv()
            field[...] += coarse(grp, lax.rem(grp + n_grp - step, n_grp)) * grp_in[step - 1]

    transport(1, field)
    out_ref[...] = land[1]
    for copy in sent:
        copy.wait_send()


def body(n_grp, n_tile, adjoint_in, departure, fraction, level_map, coarse_map):
    cols, lev = adjoint_in.shape
    half = cols // 2
    tile_self = lax.axis_index("tile")
    places = (departure % cols).astype(F32)
    offset = (departure // cols % n_tile - tile_self + REACH) % n_tile - REACH
    blank = jnp.zeros_like(places)
    meta = jnp.stack([places] + cubic_weights(fraction) + [offset.astype(F32), blank, blank], axis=1)
    vmem = pl.BlockSpec(memory_space=pltpu.VMEM)
    n_in = 1 if n_grp == 4 else n_grp - 1
    dma = pltpu.SemaphoreType.DMA
    return pl.pallas_call(
        functools.partial(kernel, n_grp, n_tile),
        out_shape=jax.ShapeDtypeStruct((cols, lev), F32),
        in_specs=[vmem] * 4,
        out_specs=vmem,
        scratch_shapes=[
            pltpu.VMEM((cols, cols), BF16),
            pltpu.VMEM((16, cols), jnp.int32),
            pltpu.VMEM((2, REMOTE + 1, half, cols), BF16),
            pltpu.VMEM((cols, 2 * lev), BF16),
            pltpu.VMEM((2, REMOTE, half, lev), F32),
            pltpu.VMEM((2, REMOTE + 1, half, lev), F32),
            pltpu.VMEM((2, REMOTE, 8, half), F32),
            pltpu.VMEM((2, REMOTE + 1, 8, half), F32),
            pltpu.VMEM((half, 2 * lev), BF16),
            pltpu.VMEM((2, cols, lev), F32),
            pltpu.VMEM((2, 8, lev), F32),
            pltpu.VMEM((2, 2, 8, lev), F32),
            pltpu.VMEM((cols, lev), F32),
            pltpu.VMEM((n_in, cols, lev), F32),
            pltpu.VMEM((cols, lev), F32),
            pltpu.VMEM((cols, lev), F32),
            dma((2, REMOTE)),
            dma((2, REMOTE)),
            dma((2, REMOTE)),
            dma((2, REMOTE)),
            dma((2, 2)),
            dma((2, 2)),
            dma((max(2, n_grp - 1), 2)),
            dma((max(2, n_grp - 1), 2)),
        ],
        compiler_params=pltpu.CompilerParams(
            collective_id=0, has_side_effects=True, vmem_limit_bytes=48 * 2 ** 20
        ),
    )(adjoint_in, meta, level_map, coarse_map.transpose(1, 2, 0))


def solution(mesh):
    return jax.shard_map(
        functools.partial(body, mesh.shape["grp"], mesh.shape["tile"]),
        mesh=mesh,
        in_specs=(
            P(("grp", "tile"), None),
            P(None, ("grp", "tile")),
            P(None, ("grp", "tile")),
            P(),
            P(),
        ),
        out_specs=P(("grp", "tile"), None),
        check_vma=False,
    )
```

profile of v0, /device:TPU:1, one launch (start us, length us, event | category | flops | bytes accessed | tf_op | source)
XLA Modules:
  0.0 78.8 jit_solution(3738010741001105418)
XLA Ops:
  0.0 0.8 fusion.14
  0.8 0.0 copy-start.3
  0.8 0.7 copy-done.3
  1.5 0.0 copy-start.1
  1.6 0.0 copy-start.2
  1.6 0.1 stack.31.meta_ref
  1.7 0.7 copy-done.1
  2.4 0.0 copy-done.2
  2.4 0.0 copy-start
  2.4 1.0 %copy-done = f32[1024,128]{1,0:T(8,128)S(1)} copy-done((f32[1024,128]{1,0:T(8,128)S(1)}, f32[1024,128]{1,0:T(8,128)}, u32[]{:S(2)}) %copy-start) | copy-done | bytes 524312
  3.4 74.6 %shard_map.55 = f32[1024,128]{1,0:T(8,128)S(1)} custom-call(f32[1024,128]{1,0:T(8,128)S(1)} %copy-done, f32[2,8,1024]{2,1,0:T(8,128)S(1)} %stack.31.meta_ref, f32[2,128,128]{2,1,0:T(8,128)S(1)} %copy-done.1, f32[4,4,128]{2,1,0:T(4,128)S(1)} %bitcast.9), custom_call_target="tpu_custom_call" | custom-call | tf_op jit(solution)/shard_map/pallas_call | solution.py:251
  78.0 0.8 %copy.11 = f32[1024,128]{1,0:T(8,128)} copy(f32[1024,128]{1,0:T(8,128)S(1)} %shard_map.55) | data formatting | bytes 1048576
  (8 shorter events, 0.1 us)
Async XLA Ops:
  0.8 0.7 copy-start.3
  1.5 0.9 %copy-start.1 = (f32[2,128,128]{2,1,0:T(8,128)S(1)}, f32[2,128,128]{2,1,0:T(8,128)}, u32[]{:S(2)}) copy-start(f32[2,128,128]{2,1,0:T(8,128)} %lm_ref.1) | copy-start | bytes 393220
  1.6 0.8 %copy-start.2 = (f32[128,4,4]{0,2,1:T(4,128)S(1)}, f32[128,4,4]{0,2,1:T(4,128)}, u32[]{:S(2)}) copy-start(f32[128,4,4]{0,2,1:T(4,128)} %param.9) | copy-start | bytes 24580
  2.4 1.0 %copy-start = (f32[1024,128]{1,0:T(8,128)S(1)}, f32[1024,128]{1,0:T(8,128)}, u32[]{:S(2)}) copy-start(f32[1024,128]{1,0:T(8,128)} %x_ref.1) | copy-start | bytes 1572868
where the time goes:
time: 79.8 us; the launch traced here: 78.8 us
  Pallas kernels  74.6 us (93%)
  local copies, waits for them, and re-layouts  3.36 us (4%)
    pallas_call x1, Pallas kernels, body(): pl.pallas_call(functools.partial(kernel, n_grp, n_tile), out_shape=jax.Sh...  74.6 us
    unnamed x9, local copies, waits for them, and re-layouts  3.2 us

commit v1 on v0

v1 whole, which is shorter than its diff:
```python
import functools

import jax
import jax.numpy as jnp
from jax import lax
from jax.experimental import pallas as pl
from jax.experimental.pallas import tpu as pltpu
from jax.sharding import PartitionSpec as P

REACH = 2
SHIFTS = (2, -2, 1, -1, 0)
REMOTE = 4
EDGE_SHIFTS = (1, -1, 2, -2, 3, -3)
CHUNKS = 4
BF16 = jnp.bfloat16
F32 = jnp.float32


def cubic_weights(a):
    return [
        -a * (1.0 - a) * (2.0 - a) / 6.0,
        (1.0 + a) * (1.0 - a) * (2.0 - a) / 2.0,
        (1.0 + a) * a * (2.0 - a) / 2.0,
        -(1.0 + a) * a * (1.0 - a) / 6.0,
    ]


def split(x):
    high = x.astype(BF16)
    return high, (x - high.astype(F32)).astype(BF16)


def dot(a, b):
    return jnp.dot(a, b, preferred_element_type=F32)


def dot_nt(a, b):
    return lax.dot_general(a, b, (((1,), (1,)), ((), ())), preferred_element_type=F32)


def kernel(
    n_grp, n_tile, x_hbm, lm_hbm, meta_ref, cm_ref, out_ref,
    x_ref, lm_ref, slots, pick, lifted, rows_out, rows_in, meta_out, meta_in, rows_hl,
    s_high, s_low, land, edge, edge_in, field, grp_in, grp_mid, grp_last,
    load_sem, rows_ss, rows_rs, meta_ss, meta_rs, edge_ss, edge_rs, grp_ss, grp_rs,
):
    cols, lev = x_ref.shape
    half = cols // 2
    grp = lax.axis_index("grp")
    tile = lax.axis_index("tile")

    def at_tile(by):
        return {"tile": lax.rem(tile + (by + n_tile), n_tile)}

    def at_grp(g):
        return {"grp": g}

    barrier = pltpu.get_barrier_semaphore()
    for by in EDGE_SHIFTS:
        pl.semaphore_signal(barrier, inc=1, device_id=at_tile(by), device_id_type=pl.DeviceIdType.MESH)
    for step in range(1, n_grp):
        pl.semaphore_signal(
            barrier, inc=1, device_id=at_grp(lax.rem(grp + step, n_grp)),
            device_id_type=pl.DeviceIdType.MESH,
        )
    loads = [
        pltpu.make_async_copy(x_hbm, x_ref, load_sem.at[0]),
        pltpu.make_async_copy(lm_hbm, lm_ref, load_sem.at[1]),
    ]
    for load in loads:
        load.start()

    sent = []
    metas = ([], [])

    def send(src, dst, ss, rs, where):
        copy = pltpu.make_async_remote_copy(
            src_ref=src, dst_ref=dst, send_sem=ss, recv_sem=rs,
            device_id=where, device_id_type=pl.DeviceIdType.MESH,
        )
        copy.start()
        sent.append(copy)
        return copy

    row8 = lax.broadcasted_iota(jnp.int32, (8, cols), 0)
    wanted = jnp.full((8, cols), -100.0, F32)
    for j, by in enumerate(SHIFTS):
        wanted = jnp.where(row8 == j, float(by), wanted)
    hot = jnp.concatenate(
        [jnp.where(wanted == meta_ref[1 - t, 5:6, :], 1.0, 0.0) for t in range(2)], axis=0
    )
    lane = 128
    r = lax.broadcasted_iota(jnp.int32, (lane, 2 * lane), 0)
    c = lax.broadcasted_iota(jnp.int32, (lane, 2 * lane), 1)
    counter = jnp.where((r < c) | (c >= lane), 1.0, 0.0).astype(BF16)
    stacked = jnp.concatenate([hot[:, i * lane : (i + 1) * lane] for i in range(cols // lane)], axis=0)
    counts = dot(stacked.astype(BF16), counter)
    total = jnp.zeros((16, lane), F32)
    for i in range(cols // lane):
        own = counts[16 * i : 16 * i + 16]
        before = own[:, :lane] + total
        total = total + own[:, lane:]
        mine = hot[:, i * lane : (i + 1) * lane] > 0.5
        slots[:, i * lane : (i + 1) * lane] = jnp.where(mine, before, -1.0).astype(jnp.int32)

    block = 128

    def build_pick(t, j):
        @pl.loop(0, half // block)
        def _(i):
            r = lax.broadcasted_iota(jnp.int32, (block, cols), 0) + i * block
            hit = r == slots[8 * t + j : 8 * t + j + 1, :]
            pick[t, j, pl.ds(pl.multiple_of(i * block, block), block), :] = jnp.where(hit, 1.0, 0.0).astype(BF16)

    def do_meta(t, j):
        whole = meta_ref[1 - t]
        a = whole.astype(BF16)
        rest = whole - a.astype(F32)
        parts = jnp.concatenate([a.astype(F32), rest], axis=0).astype(BF16)
        got = dot_nt(parts, pick[t, j])
        packed = got[:8] + got[8:]
        if j == REMOTE:
            meta_in[t, j] = packed
        else:
            meta_out[t, j] = packed
            metas[t].append(
                send(meta_out.at[t, j], meta_in.at[t, j], meta_ss.at[t, j], meta_rs.at[t, j], at_tile(SHIFTS[j]))
            )

    def build_spread(t, j):
        if j < REMOTE:
            metas[t][j].wait_recv()
        size = 128

        @pl.loop(0, cols // size)
        def _(i):
            cells = lax.broadcasted_iota(jnp.int32, (size, half), 0) + i * size
            place = meta_in[t, j, 0:1, :].astype(jnp.int32)
            value = jnp.zeros((size, half), F32)
            for k in range(4):
                value = jnp.where(cells == place + (k - 1), meta_in[t, j, 1 + k : 2 + k, :], value)
            high, low = split(value)
            at = pl.ds(pl.multiple_of(i * size, size), size)
            s_high[j, at, :] = high
            s_low[j, at, :] = low

    def deposit(t, j, first):
        high, low = split(rows_in[t, j])
        rows_hl[:, :lev] = high
        rows_hl[:, lev:] = low
        size = 512

        @pl.loop(0, cols // size)
        def _(i):
            at = pl.ds(pl.multiple_of(i * size, size), size)
            wide = dot(s_high[j, at, :], rows_hl[...])
            part = wide[:, :lev] + wide[:, lev:] + dot(s_low[j, at, :], rows_hl[:, :lev])
            if first:
                land[t, at, :] = part
            else:
                land[t, at, :] += part

    def send_edges(t):
        place = meta_ref[1 - t, 0:1, :]
        w = [meta_ref[1 - t, 1 + k : 2 + k, :] for k in range(4)]
        offset = meta_ref[1 - t, 5:6, :]
        last = place == float(cols - 1)
        forward = jnp.where(last, w[2], jnp.where(place == float(cols - 2), w[3], 0.0))
        forward2 = jnp.where(last, w[3], 0.0)
        backward = jnp.where(place == 0.0, w[0], 0.0)
        blocks = []
        for by in EDGE_SHIFTS + (0, 0):
            near = offset == float(by - 1)
            value = jnp.where(row8 == 0, jnp.where(near, forward, 0.0), 0.0)
            value = jnp.where(row8 == 1, jnp.where(near, forward2, 0.0), value)
            value = jnp.where(row8 == 2, jnp.where(offset == float(by + 1), backward, 0.0), value)
            blocks.append(value)
        high, low = split(jnp.concatenate(blocks, axis=0))
        wide = dot(high, lifted[...])
        sums = wide[:, :lev] + wide[:, lev:] + dot(low, lifted[:, :lev])
        copies = []
        for n, by in enumerate(EDGE_SHIFTS):
            edge[t, n] = sums[8 * n : 8 * n + 8]
            copies.append(send(edge.at[t, n], edge_in.at[t, n], edge_ss.at[t, n], edge_rs.at[t, n], at_tile(by)))
        n = len(EDGE_SHIFTS)
        edge[t, n] = sums[8 * n : 8 * n + 8]
        return copies

    def transport(t, src):
        m_high, m_low = split(lm_ref[1 - t])
        f_high, f_low = split(src[...])
        lift = dot_nt(f_high, m_high) + dot_nt(f_low, m_high) + dot_nt(f_high, m_low)
        l_high, l_low = split(lift)
        lifted[:, :lev] = l_high
        lifted[:, lev:] = l_low
        copies = []
        for j in range(REMOTE + 1):
            if t == 0:
                build_pick(t, j)
                if j == 0:
                    pl.semaphore_wait(barrier, len(EDGE_SHIFTS) + n_grp - 1)
                do_meta(t, j)
            both = dot(pick[t, j], lifted[...])
            packed = both[:, :lev] + both[:, lev:]
            if j < REMOTE:
                rows_out[t, j] = packed
                copies.append(
                    send(rows_out.at[t, j], rows_in.at[t, j], rows_ss.at[t, j], rows_rs.at[t, j], at_tile(SHIFTS[j]))
                )
            else:
                rows_in[t, j] = packed
        edges = send_edges(t)
        if t == 0:
            build_spread(t, REMOTE)
        deposit(t, REMOTE, True)
        if t == 0:
            for j in range(REMOTE):
                build_spread(t, j)
        for j in (2, 3, 0, 1):
            copies[j].wait_recv()
            deposit(t, j, False)
        sums = edge[t, len(edges)]
        for n, copy in enumerate(edges):
            copy.wait_recv()
            sums = sums + edge_in[t, n]
        r = lax.broadcasted_iota(jnp.int32, (8, lev), 0)
        land[t, 0:8, :] += jnp.where(r < 2, sums, 0.0)
        land[t, cols - 8 : cols, :] += jnp.where(r == 7, sums[2:3], 0.0)

    def prepare():
        for j in range(REMOTE + 1):
            build_pick(1, j)
            do_meta(1, j)

    def prepare_spread():
        for j in range(REMOTE + 1):
            build_spread(1, j)

    def coarse(b, e):
        return cm_ref[b, pl.ds(e, 1), :]

    for load in loads:
        load.wait()
    transport(0, x_ref)

    if n_grp == 4:
        flip_x = grp + 1 - 2 * lax.rem(grp, 2)
        flip_y = lax.rem(grp + 2, 4)
        chunks = []
        for n in range(CHUNKS):
            near, far = ((flip_x, flip_y), (flip_y, flip_x))[n % 2]
            chunks.append((n, pl.ds(n * (cols // CHUNKS), cols // CHUNKS), near, far))
        firsts = []
        lasts = []
        for n, at, near, far in chunks:
            firsts.append(send(land.at[0, at], grp_in.at[0, at], grp_ss.at[0, n], grp_rs.at[0, n], at_grp(near)))
        prepare()
        for n, at, near, far in chunks:
            firsts[n].wait_recv()
            grp_mid[at, :] = coarse(far, grp) * land[0, at, :] + coarse(far, near) * grp_in[0, at, :]
            lasts.append(send(grp_mid.at[at], grp_last.at[at], grp_ss.at[1, n], grp_rs.at[1, n], at_grp(far)))
        for n, at, near, far in chunks:
            field[at, :] = coarse(grp, grp) * land[0, at, :] + coarse(grp, near) * grp_in[0, at, :]
        prepare_spread()
        for n, at, near, far in chunks:
            lasts[n].wait_recv()
            field[at, :] += grp_last[at, :]
    else:
        copies = []
        for step in range(1, n_grp):
            to = lax.rem(grp + step, n_grp)
            copies.append(
                send(land.at[0], grp_in.at[step - 1], grp_ss.at[step - 1, 0], grp_rs.at[step - 1, 0], at_grp(to))
            )
        prepare()
        prepare_spread()
        field[...] = coarse(grp, grp) * land[0]
        for step in range(1, n_grp):
            copies[step - 1].wait_recv()
            field[...] += coarse(grp, lax.rem(grp + n_grp - step, n_grp)) * grp_in[step - 1]

    transport(1, field)
    out_ref[...] = land[1]
    for copy in sent:
        copy.wait_send()


def body(n_grp, n_tile, adjoint_in, departure, fraction, level_map, coarse_map):
    cols, lev = adjoint_in.shape
    half = cols // 2
    tile_self = lax.axis_index("tile")
    places = (departure % cols).astype(F32)
    offset = (departure // cols % n_tile - tile_self + REACH) % n_tile - REACH
    blank = jnp.zeros_like(places)
    meta = jnp.stack([places] + cubic_weights(fraction) + [offset.astype(F32), blank, blank], axis=1)
    vmem = pl.BlockSpec(memory_space=pltpu.VMEM)
    n_in = 1 if n_grp == 4 else n_grp - 1
    dma = pltpu.SemaphoreType.DMA
    return pl.pallas_call(
        functools.partial(kernel, n_grp, n_tile),
        out_shape=jax.ShapeDtypeStruct((cols, lev), F32),
        in_specs=[pl.BlockSpec(memory_space=pl.ANY)] * 2 + [vmem] * 2,
        out_specs=vmem,
        scratch_shapes=[
            pltpu.VMEM((cols, lev), F32),
            pltpu.VMEM(level_map.shape, F32),
            pltpu.VMEM((16, cols), jnp.int32),
            pltpu.VMEM((2, REMOTE + 1, half, cols), BF16),
            pltpu.VMEM((cols, 2 * lev), BF16),
            pltpu.VMEM((2, REMOTE, half, lev), F32),
            pltpu.VMEM((2, REMOTE + 1, half, lev), F32),
            pltpu.VMEM((2, REMOTE, 8, half), F32),
            pltpu.VMEM((2, REMOTE + 1, 8, half), F32),
            pltpu.VMEM((half, 2 * lev), BF16),
            pltpu.VMEM((REMOTE + 1, cols, half), BF16),
            pltpu.VMEM((REMOTE + 1, cols, half), BF16),
            pltpu.VMEM((2, cols, lev), F32),
            pltpu.VMEM((2, len(EDGE_SHIFTS) + 1, 8, lev), F32),
            pltpu.VMEM((2, len(EDGE_SHIFTS), 8, lev), F32),
            pltpu.VMEM((cols, lev), F32),
            pltpu.VMEM((n_in, cols, lev), F32),
            pltpu.VMEM((cols, lev), F32),
            pltpu.VMEM((cols, lev), F32),
            dma((2,)),
            dma((2, REMOTE)),
            dma((2, REMOTE)),
            dma((2, REMOTE)),
            dma((2, REMOTE)),
            dma((2, len(EDGE_SHIFTS))),
            dma((2, len(EDGE_SHIFTS))),
            dma((max(2, n_grp - 1), CHUNKS)),
            dma((max(2, n_grp - 1), CHUNKS)),
        ],
        compiler_params=pltpu.CompilerParams(
            collective_id=0, has_side_effects=True, vmem_limit_bytes=48 * 2 ** 20
        ),
    )(adjoint_in, level_map, meta, coarse_map.transpose(1, 2, 0))


def solution(mesh):
    return jax.shard_map(
        functools.partial(body, mesh.shape["grp"], mesh.shape["tile"]),
        mesh=mesh,
        in_specs=(
            P(("grp", "tile"), None),
            P(None, ("grp", "tile")),
            P(None, ("grp", "tile")),
            P(),
            P(),
        ),
        out_specs=P(("grp", "tile"), None),
        check_vma=False,
    )
```

time: 79.8 us -> 70.8 us (0.89)
  the two profiles are of different devices: /device:TPU:1 before, /device:TPU:0 now
where the time goes in v1:
time: 70.8 us; the launch traced here: 70.5 us
  Pallas kernels  66.3 us (94%)
  local copies, waits for them, and re-layouts  3.36 us (5%)
  other arithmetic  0.79 us (1%)
    pallas_call x1, Pallas kernels, body(): pl.pallas_call(functools.partial(kernel, n_grp, n_tile), out_shape=jax.Sh...  66.3 us
    unnamed x9, local copies, waits for them, and re-layouts  3.2 us

profile of v1, /device:TPU:0, one launch (start us, length us, event | category | flops | bytes accessed | tf_op | source)
XLA Modules:
  0.0 70.5 jit_solution(17298724640520621127)
XLA Ops:
  0.0 0.8 %fusion.14 = (f32[2,1024]{1,0:T(2,128)S(1)}, f32[2,1,1024]{2,0,1:T(2,128)S(1)}) fusion(s32[2,1024]{1,0:T(2,128)} %param.6, s32[]{:T(128)S(6)} %axis_index.12), kind=kLoop, calls=%fused_computation.28 | loop fusion | flops 94208 | bytes 24580 | tf_op jit(solution)/shard_map/convert_element_type | solution.py:295
  0.8 0.0 copy-start.3
  0.8 0.7 copy-done.3
  1.5 0.0 copy-start.1
  1.6 0.0 copy-start.2
  1.6 0.1 stack.31.meta_ref
  1.7 0.7 copy-done.1
  2.4 0.0 copy-done.2
  2.4 0.0 copy-start
  2.4 1.0 %copy-done = f32[1024,128]{1,0:T(8,128)S(1)} copy-done((f32[1024,128]{1,0:T(8,128)S(1)}, f32[1024,128]{1,0:T(8,128)}, u32[]{:S(2)}) %copy-start) | copy-done | bytes 524312
  3.4 66.3 %shard_map.55 = f32[1024,128]{1,0:T(8,128)S(1)} custom-call(f32[1024,128]{1,0:T(8,128)S(1)} %copy-done, f32[2,128,128]{2,1,0:T(8,128)S(1)} %copy-done.1, f32[2,8,1024]{2,1,0:T(8,128)S(1)} %stack.31.meta_ref, f32[4,4,128]{2,1,0:T(4,128)S(1)} %bitcast.9), custom_call_target="tpu_custom_call" | custom-call | tf_op jit(solution)/shard_map/pallas_call | solution.py:299
  69.7 0.8 %copy.11 = f32[1024,128]{1,0:T(8,128)} copy(f32[1024,128]{1,0:T(8,128)S(1)} %shard_map.55) | data formatting | bytes 1048576
  (8 shorter events, 0.1 us)
Async XLA Ops:
  0.8 0.7 copy-start.3
  1.5 0.9 %copy-start.1 = (f32[2,128,128]{2,1,0:T(8,128)S(1)}, f32[2,128,128]{2,1,0:T(8,128)}, u32[]{:S(2)}) copy-start(f32[2,128,128]{2,1,0:T(8,128)} %lm_hbm.1) | copy-start | bytes 393220
  1.6 0.8 %copy-start.2 = (f32[128,4,4]{0,2,1:T(4,128)S(1)}, f32[128,4,4]{0,2,1:T(4,128)}, u32[]{:S(2)}) copy-start(f32[128,4,4]{0,2,1:T(4,128)} %param.9) | copy-start | bytes 24580
  2.4 1.0 %copy-start = (f32[1024,128]{1,0:T(8,128)S(1)}, f32[1024,128]{1,0:T(8,128)}, u32[]{:S(2)}) copy-start(f32[1024,128]{1,0:T(8,128)} %x_hbm.1) | copy-start | bytes 1572868

commit v2 on v1

--- a/solution.py
+++ b/solution.py
@@ -12,6 +12,7 @@
 REMOTE = 4
 EDGE_SHIFTS = (1, -1, 2, -2, 3, -3)
 CHUNKS = 4
+ARRIVE = (2, 3, 0, 1)
 BF16 = jnp.bfloat16
 F32 = jnp.float32
 
@@ -39,9 +40,10 @@
 
 
 def kernel(
-    n_grp, n_tile, x_hbm, lm_hbm, meta_ref, cm_ref, out_ref,
-    x_ref, lm_ref, slots, pick, lifted, rows_out, rows_in, meta_out, meta_in, rows_hl,
-    s_high, s_low, land, edge, edge_in, field, grp_in, grp_mid, grp_last,
+    n_grp, n_tile, x_hbm, dep_hbm, frac_hbm, lm_hbm, cm_hbm, out_ref,
+    x_ref, dep_ref, frac_ref, lm_ref, cm_ref, meta_ref,
+    slots, pick, lifted, rows_out, rows_in, meta_out, meta_in, rows_hl,
+    s_high, s_low, land, edge, edge_in, field, grp_out, grp_in, grp_mid, grp_last,
     load_sem, rows_ss, rows_rs, meta_ss, meta_rs, edge_ss, edge_rs, grp_ss, grp_rs,
 ):
     cols, lev = x_ref.shape
@@ -63,12 +65,20 @@
             barrier, inc=1, device_id=at_grp(lax.rem(grp + step, n_grp)),
             device_id_type=pl.DeviceIdType.MESH,
         )
-    loads = [
-        pltpu.make_async_copy(x_hbm, x_ref, load_sem.at[0]),
-        pltpu.make_async_copy(lm_hbm, lm_ref, load_sem.at[1]),
-    ]
+    pairs = ((dep_hbm, dep_ref), (frac_hbm, frac_ref), (x_hbm, x_ref), (lm_hbm, lm_ref), (cm_hbm, cm_ref))
+    loads = [pltpu.make_async_copy(src, dst, load_sem.at[n]) for n, (src, dst) in enumerate(pairs)]
     for load in loads:
         load.start()
+    for load in loads[:2]:
+        load.wait()
+    departure = dep_ref[...]
+    target = (departure >> (cols.bit_length() - 1)) & (n_tile - 1)
+    offset = ((target - tile + REACH) & (n_tile - 1)) - REACH
+    values = [(departure & (cols - 1)).astype(F32)] + cubic_weights(frac_ref[...]) + [offset.astype(F32)]
+    meta_ref[...] = jnp.zeros_like(meta_ref)
+    for n, value in enumerate(values):
+        for t in range(2):
+            meta_ref[t, n : n + 1, :] = value[t : t + 1]
 
     sent = []
     metas = ([], [])
@@ -144,21 +154,47 @@
             s_high[j, at, :] = high
             s_low[j, at, :] = low
 
-    def deposit(t, j, first):
-        high, low = split(rows_in[t, j])
-        rows_hl[:, :lev] = high
-        rows_hl[:, lev:] = low
+    part_lev = lev // 2
+
+    def swap(x):
+        return pltpu.roll(x, part_lev, 1)
+
+    def left(shape):
+        return lax.broadcasted_iota(jnp.int32, shape, 1) < part_lev
+
+    def twice(x, q):
+        own = x[:, q * part_lev : (q + 1) * part_lev]
+        return jnp.concatenate([own, own], axis=1)
+
+    def deposit(t, q, j, first):
+        both = rows_in[t, q, j]
+        high = both.astype(BF16).astype(F32)
+        low = both - high
+        on_left = left(both.shape)
+        rows_hl[: half // 2, :] = jnp.where(on_left, high, swap(low)).astype(BF16)
+        rows_hl[half // 2 :, :] = jnp.where(on_left, swap(high), low).astype(BF16)
         size = 512
 
         @pl.loop(0, cols // size)
         def _(i):
             at = pl.ds(pl.multiple_of(i * size, size), size)
-            wide = dot(s_high[j, at, :], rows_hl[...])
-            part = wide[:, :lev] + wide[:, lev:] + dot(s_low[j, at, :], rows_hl[:, :lev])
+            part = dot(s_high[j, at, :], rows_hl[...]) + dot(s_low[j, at, :], rows_hl[...])
             if first:
-                land[t, at, :] = part
+                land[q, at, :] = part
             else:
-                land[t, at, :] += part
+                land[q, at, :] += part
+
+    def close(t, q, edges):
+        land[q] = land[q] + swap(land[q])
+        sums = edge[t, len(edges)]
+        for n, copy in enumerate(edges):
+            if q == 0:
+                copy.wait_recv()
+            sums = sums + edge_in[t, n]
+        sums = twice(sums, q)
+        r = lax.broadcasted_iota(jnp.int32, (8, lev), 0)
+        land[q, 0:8, :] += jnp.where(r < 2, sums, 0.0)
+        land[q, cols - 8 : cols, :] += jnp.where(r == 7, sums[2:3], 0.0)
 
     def send_edges(t):
         place = meta_ref[1 - t, 0:1, :]
@@ -186,14 +222,24 @@
         edge[t, n] = sums[8 * n : 8 * n + 8]
         return copies
 
-    def transport(t, src):
+    def transport(t, whole, exchange_first, exchange_last):
         m_high, m_low = split(lm_ref[1 - t])
-        f_high, f_low = split(src[...])
+        f_high, f_low = split(whole)
         lift = dot_nt(f_high, m_high) + dot_nt(f_low, m_high) + dot_nt(f_high, m_low)
         l_high, l_low = split(lift)
         lifted[:, :lev] = l_high
         lifted[:, lev:] = l_low
-        copies = []
+        on_left = left((half // 2, lev))
+        copies = ([], [])
+
+        def send_rows(q, j):
+            copies[q].append(
+                send(
+                    rows_out.at[t, q, j], rows_in.at[t, q, j], rows_ss.at[t, q, j], rows_rs.at[t, q, j],
+                    at_tile(SHIFTS[j]),
+                )
+            )
+
         for j in range(REMOTE + 1):
             if t == 0:
                 build_pick(t, j)
@@ -202,85 +248,112 @@
                 do_meta(t, j)
             both = dot(pick[t, j], lifted[...])
             packed = both[:, :lev] + both[:, lev:]
+            top, bottom = packed[: half // 2], packed[half // 2 :]
+            into = rows_out if j < REMOTE else rows_in
+            into[t, 0, j] = jnp.where(on_left, top, swap(bottom))
+            into[t, 1, j] = jnp.where(on_left, swap(top), bottom)
             if j < REMOTE:
-                rows_out[t, j] = packed
-                copies.append(
-                    send(rows_out.at[t, j], rows_in.at[t, j], rows_ss.at[t, j], rows_rs.at[t, j], at_tile(SHIFTS[j]))
-                )
-            else:
-                rows_in[t, j] = packed
+                send_rows(0, j)
         edges = send_edges(t)
+        for j in range(REMOTE):
+            send_rows(1, j)
         if t == 0:
             build_spread(t, REMOTE)
-        deposit(t, REMOTE, True)
+        for q in range(2):
+            deposit(t, q, REMOTE, True)
         if t == 0:
             for j in range(REMOTE):
                 build_spread(t, j)
-        for j in (2, 3, 0, 1):
-            copies[j].wait_recv()
-            deposit(t, j, False)
-        sums = edge[t, len(edges)]
-        for n, copy in enumerate(edges):
-            copy.wait_recv()
-            sums = sums + edge_in[t, n]
-        r = lax.broadcasted_iota(jnp.int32, (8, lev), 0)
-        land[t, 0:8, :] += jnp.where(r < 2, sums, 0.0)
-        land[t, cols - 8 : cols, :] += jnp.where(r == 7, sums[2:3], 0.0)
-
-    def prepare():
+        for q in range(2):
+            for j in ARRIVE:
+                copies[q][j].wait_recv()
+                deposit(t, q, j, False)
+            close(t, q, edges)
+            (exchange_first, exchange_last)[q]()
+
+    def coarse(b, e, q):
+        return twice(cm_ref[b, pl.ds(e, 1), :], q)
+
+    flip_x = grp + 1 - 2 * lax.rem(grp, 2)
+    flip_y = lax.rem(grp + 2, n_grp)
+    chunks = []
+    for n in range(CHUNKS):
+        near, far = ((flip_x, flip_y), (flip_y, flip_x))[n % 2]
+        chunks.append((n, pl.ds(n * (half // CHUNKS), half // CHUNKS), near, far))
+    firsts = ([], [])
+    lasts = ([], [])
+
+    def pack_part(q):
+        grp_out[q] = jnp.where(left((half, lev)), land[q, :half, :], land[q, half:, :])
+
+    def start(q):
+        pack_part(q)
+        for n, at, near, far in chunks:
+            firsts[q].append(
+                send(grp_out.at[q, at], grp_in.at[q, 0, at], grp_ss.at[q, 0, n], grp_rs.at[q, 0, n], at_grp(near))
+            )
+
+    def pass_on(q):
+        for n, at, near, far in chunks:
+            firsts[q][n].wait_recv()
+            grp_mid[q, at, :] = coarse(far, grp, q) * grp_out[q, at, :] + coarse(far, near, q) * grp_in[q, 0, at, :]
+            lasts[q].append(
+                send(grp_mid.at[q, at], grp_last.at[q, at], grp_ss.at[q, 1, n], grp_rs.at[q, 1, n], at_grp(far))
+            )
+        for n, at, near, far in chunks:
+            field[q, at, :] = coarse(grp, grp, q) * grp_out[q, at, :] + coarse(grp, near, q) * grp_in[q, 0, at, :]
+
+    def finish(q):
+        for n, at, near, far in chunks:
+            lasts[q][n].wait_recv()
+            field[q, at, :] += grp_last[q, at, :]
+
+    def start_any(q):
+        pack_part(q)
+        for step in range(1, n_grp):
+            to = lax.rem(grp + step, n_grp)
+            firsts[q].append(
+                send(grp_out.at[q], grp_in.at[q, step - 1], grp_ss.at[q, step - 1, 0], grp_rs.at[q, step - 1, 0], at_grp(to))
+            )
+
+    def finish_any(q):
+        field[q] = coarse(grp, grp, q) * grp_out[q]
+        for step in range(1, n_grp):
+            firsts[q][step - 1].wait_recv()
+            field[q] += coarse(grp, lax.rem(grp + n_grp - step, n_grp), q) * grp_in[q, step - 1]
+
+    square = n_grp == 4
+
+    def exchange_first():
+        (start if square else start_any)(0)
         for j in range(REMOTE + 1):
             build_pick(1, j)
+        if square:
+            pass_on(0)
+
+    def exchange_last():
+        (start if square else start_any)(1)
+        for j in range(REMOTE + 1):
             do_meta(1, j)
-
-    def prepare_spread():
+        if square:
+            pass_on(1)
         for j in range(REMOTE + 1):
             build_spread(1, j)
-
-    def coarse(b, e):
-        return cm_ref[b, pl.ds(e, 1), :]
-
-    for load in loads:
+        for q in range(2):
+            (finish if square else finish_any)(q)
+
+    def nothing():
+        pass
+
+    for load in loads[2:]:
         load.wait()
-    transport(0, x_ref)
-
-    if n_grp == 4:
-        flip_x = grp + 1 - 2 * lax.rem(grp, 2)
-        flip_y = lax.rem(grp + 2, 4)
-        chunks = []
-        for n in range(CHUNKS):
-            near, far = ((flip_x, flip_y), (flip_y, flip_x))[n % 2]
-            chunks.append((n, pl.ds(n * (cols // CHUNKS), cols // CHUNKS), near, far))
-        firsts = []
-        lasts = []
-        for n, at, near, far in chunks:
-            firsts.append(send(land.at[0, at], grp_in.at[0, at], grp_ss.at[0, n], grp_rs.at[0, n], at_grp(near)))
-        prepare()
-        for n, at, near, far in chunks:
-            firsts[n].wait_recv()
-            grp_mid[at, :] = coarse(far, grp) * land[0, at, :] + coarse(far, near) * grp_in[0, at, :]
-            lasts.append(send(grp_mid.at[at], grp_last.at[at], grp_ss.at[1, n], grp_rs.at[1, n], at_grp(far)))
-        for n, at, near, far in chunks:
-            field[at, :] = coarse(grp, grp) * land[0, at, :] + coarse(grp, near) * grp_in[0, at, :]
-        prepare_spread()
-        for n, at, near, far in chunks:
-            lasts[n].wait_recv()
-            field[at, :] += grp_last[at, :]
-    else:
-        copies = []
-        for step in range(1, n_grp):
-            to = lax.rem(grp + step, n_grp)
-            copies.append(
-                send(land.at[0], grp_in.at[step - 1], grp_ss.at[step - 1, 0], grp_rs.at[step - 1, 0], at_grp(to))
-            )
-        prepare()
-        prepare_spread()
-        field[...] = coarse(grp, grp) * land[0]
-        for step in range(1, n_grp):
-            copies[step - 1].wait_recv()
-            field[...] += coarse(grp, lax.rem(grp + n_grp - step, n_grp)) * grp_in[step - 1]
-
-    transport(1, field)
-    out_ref[...] = land[1]
+    transport(0, x_ref[...], exchange_first, exchange_last)
+    on_left = left((half, lev))
+    whole = jnp.concatenate(
+        [jnp.where(on_left, field[0], swap(field[1])), jnp.where(on_left, swap(field[0]), field[1])], axis=0
+    )
+    transport(1, whole, nothing, nothing)
+    out_ref[...] = jnp.where(left((cols, lev)), land[0], land[1])
     for copy in sent:
         copy.wait_send()
 
@@ -288,53 +361,52 @@
 def body(n_grp, n_tile, adjoint_in, departure, fraction, level_map, coarse_map):
     cols, lev = adjoint_in.shape
     half = cols // 2
-    tile_self = lax.axis_index("tile")
-    places = (departure % cols).astype(F32)
-    offset = (departure // cols % n_tile - tile_self + REACH) % n_tile - REACH
-    blank = jnp.zeros_like(places)
-    meta = jnp.stack([places] + cubic_weights(fraction) + [offset.astype(F32), blank, blank], axis=1)
-    vmem = pl.BlockSpec(memory_space=pltpu.VMEM)
     n_in = 1 if n_grp == 4 else n_grp - 1
     dma = pltpu.SemaphoreType.DMA
     return pl.pallas_call(
         functools.partial(kernel, n_grp, n_tile),
         out_shape=jax.ShapeDtypeStruct((cols, lev), F32),
-        in_specs=[pl.BlockSpec(memory_space=pl.ANY)] * 2 + [vmem] * 2,
-        out_specs=vmem,
+        in_specs=[pl.BlockSpec(memory_space=pltpu.HBM)] * 5,
+        out_specs=pl.BlockSpec(memory_space=pltpu.VMEM),
         scratch_shapes=[
             pltpu.VMEM((cols, lev), F32),
+            pltpu.VMEM((2, cols), jnp.int32),
+            pltpu.VMEM((2, cols), F32),
             pltpu.VMEM(level_map.shape, F32),
+            pltpu.VMEM((n_grp, n_grp, lev), F32),
+            pltpu.VMEM((2, 8, cols), F32),
             pltpu.VMEM((16, cols), jnp.int32),
             pltpu.VMEM((2, REMOTE + 1, half, cols), BF16),
             pltpu.VMEM((cols, 2 * lev), BF16),
-            pltpu.VMEM((2, REMOTE, half, lev), F32),
-            pltpu.VMEM((2, REMOTE + 1, half, lev), F32),
+            pltpu.VMEM((2, 2, REMOTE, half // 2, lev), F32),
+            pltpu.VMEM((2, 2, REMOTE + 1, half // 2, lev), F32),
             pltpu.VMEM((2, REMOTE, 8, half), F32),
             pltpu.VMEM((2, REMOTE + 1, 8, half), F32),
-            pltpu.VMEM((half, 2 * lev), BF16),
+            pltpu.VMEM((half, lev), BF16),
             pltpu.VMEM((REMOTE + 1, cols, half), BF16),
             pltpu.VMEM((REMOTE + 1, cols, half), BF16),
             pltpu.VMEM((2, cols, lev), F32),
             pltpu.VMEM((2, len(EDGE_SHIFTS) + 1, 8, lev), F32),
             pltpu.VMEM((2, len(EDGE_SHIFTS), 8, lev), F32),
-            pltpu.VMEM((cols, lev), F32),
-            pltpu.VMEM((n_in, cols, lev), F32),
-            pltpu.VMEM((cols, lev), F32),
-            pltpu.VMEM((cols, lev), F32),
-            dma((2,)),
-            dma((2, REMOTE)),
-            dma((2, REMOTE)),
+            pltpu.VMEM((2, half, lev), F32),
+            pltpu.VMEM((2, half, lev), F32),
+            pltpu.VMEM((2, n_in, half, lev), F32),
+            pltpu.VMEM((2, half, lev), F32),
+            pltpu.VMEM((2, half, lev), F32),
+            dma((5,)),
+            dma((2, 2, REMOTE)),
+            dma((2, 2, REMOTE)),
             dma((2, REMOTE)),
             dma((2, REMOTE)),
             dma((2, len(EDGE_SHIFTS))),
             dma((2, len(EDGE_SHIFTS))),
-            dma((max(2, n_grp - 1), CHUNKS)),
-            dma((max(2, n_grp - 1), CHUNKS)),
+            dma((2, max(2, n_grp - 1), CHUNKS)),
+            dma((2, max(2, n_grp - 1), CHUNKS)),
         ],
         compiler_params=pltpu.CompilerParams(
             collective_id=0, has_side_effects=True, vmem_limit_bytes=48 * 2 ** 20
         ),
-    )(adjoint_in, level_map, meta, coarse_map.transpose(1, 2, 0))
+    )(adjoint_in, departure, fraction, level_map, coarse_map.transpose(1, 2, 0))
 
 
 def solution(mesh):

time: 70.8 us -> 71.3 us (level)
  the two profiles are of different devices: /device:TPU:0 before, /device:TPU:1 now
where the time goes in v2:
time: 71.3 us; the launch traced here: 70.6 us
  Pallas kernels  65.7 us (92%)
  local copies, waits for them, and re-layouts  4.83 us (7%)
    pallas_call x1, Pallas kernels, body(): pl.pallas_call(functools.partial(kernel, n_grp, n_tile), out_shape=jax.Sh...  65.7 us
    unnamed x11, local copies, waits for them, and re-layouts  4.83 us

profile of v2, /device:TPU:1, one launch (start us, length us, event | category | flops | bytes accessed | tf_op | source)
XLA Modules:
  0.0 70.6 jit_solution(16883530702120903184)
XLA Ops:
  0.0 0.0 copy-start
  0.0 1.0 %copy-done = f32[1024,128]{1,0:T(8,128)S(1)} copy-done((f32[1024,128]{1,0:T(8,128)S(1)}, f32[1024,128]{1,0:T(8,128)}, u32[]{:S(2)}) %copy-start) | copy-done | bytes 524312
  1.0 0.0 copy-start.1
  1.0 0.9 %copy-done.1 = f32[2,128,128]{2,1,0:T(8,128)S(1)} copy-done((f32[2,128,128]{2,1,0:T(8,128)S(1)}, f32[2,128,128]{2,1,0:T(8,128)}, u32[]{:S(2)}) %copy-start.1) | copy-done | bytes 131096
  1.9 0.0 copy-start.2
  1.9 0.7 copy-done.2
  2.6 0.0 copy-start.3
  2.6 0.7 copy-done.3
  3.3 0.0 copy-start.4
  3.3 0.7 copy-done.4
  4.0 65.7 %shard_map.55 = f32[1024,128]{1,0:T(8,128)S(1)} custom-call(f32[1024,128]{1,0:T(8,128)S(1)} %copy-done, s32[2,1024]{1,0:T(2,128)S(1)} %copy-done.2, f32[2,1024]{1,0:T(2,128)S(1)} %copy-done.3, f32[2,128,128]{2,1,0:T(8,128)S(1)} %copy-done.1, f32[4,4,128]{2,1,0:T(4,128)S(1)} %bitcast.1), custom_call_target="tpu_custom_call" | custom-call | tf_op jit(solution)/shard_map/pallas_call | solution.py:366
  69.8 0.8 %copy.7 = f32[1024,128]{1,0:T(8,128)} copy(f32[1024,128]{1,0:T(8,128)S(1)} %shard_map.55) | data formatting | bytes 1048576
Async XLA Ops:
  0.0 1.0 %copy-start = (f32[1024,128]{1,0:T(8,128)S(1)}, f32[1024,128]{1,0:T(8,128)}, u32[]{:S(2)}) copy-start(f32[1024,128]{1,0:T(8,128)} %x_hbm.1) | copy-start | bytes 1572868
  1.0 0.9 %copy-start.1 = (f32[2,128,128]{2,1,0:T(8,128)S(1)}, f32[2,128,128]{2,1,0:T(8,128)}, u32[]{:S(2)}) copy-start(f32[2,128,128]{2,1,0:T(8,128)} %lm_hbm.1) | copy-start | bytes 393220
  1.9 0.7 copy-start.2
  2.6 0.7 copy-start.3
  3.3 0.7 copy-start.4

commit v3 on v2

--- a/solution.py
+++ b/solution.py
@@ -81,6 +81,7 @@
             meta_ref[t, n : n + 1, :] = value[t : t + 1]
 
     sent = []
+    left_already = []
     metas = ([], [])
 
     def send(src, dst, ss, rs, where):
@@ -230,10 +231,10 @@
         lifted[:, :lev] = l_high
         lifted[:, lev:] = l_low
         on_left = left((half // 2, lev))
-        copies = ([], [])
+        copies = ({}, {})
 
         def send_rows(q, j):
-            copies[q].append(
+            copies[q][j] = (
                 send(
                     rows_out.at[t, q, j], rows_in.at[t, q, j], rows_ss.at[t, q, j], rows_rs.at[t, q, j],
                     at_tile(SHIFTS[j]),
@@ -245,7 +246,6 @@
                 build_pick(t, j)
                 if j == 0:
                     pl.semaphore_wait(barrier, len(EDGE_SHIFTS) + n_grp - 1)
-                do_meta(t, j)
             both = dot(pick[t, j], lifted[...])
             packed = both[:, :lev] + both[:, lev:]
             top, bottom = packed[: half // 2], packed[half // 2 :]
@@ -254,9 +254,10 @@
             into[t, 1, j] = jnp.where(on_left, swap(top), bottom)
             if j < REMOTE:
                 send_rows(0, j)
+        if t == 0:
+            for j in range(REMOTE + 1):
+                do_meta(t, j)
         edges = send_edges(t)
-        for j in range(REMOTE):
-            send_rows(1, j)
         if t == 0:
             build_spread(t, REMOTE)
         for q in range(2):
@@ -264,6 +265,10 @@
         if t == 0:
             for j in range(REMOTE):
                 build_spread(t, j)
+        for j in (2, 3, 0, 1):
+            copies[0][j].wait_send()
+            left_already.append(id(copies[0][j]))
+            send_rows(1, j)
         for q in range(2):
             for j in ARRIVE:
                 copies[q][j].wait_recv()
@@ -330,14 +335,16 @@
             build_pick(1, j)
         if square:
             pass_on(0)
+        for j in range(REMOTE + 1):
+            do_meta(1, j)
 
     def exchange_last():
         (start if square else start_any)(1)
-        for j in range(REMOTE + 1):
-            do_meta(1, j)
+        for j in (REMOTE, 0):
+            build_spread(1, j)
         if square:
             pass_on(1)
-        for j in range(REMOTE + 1):
+        for j in range(1, REMOTE):
             build_spread(1, j)
         for q in range(2):
             (finish if square else finish_any)(q)
@@ -355,7 +362,8 @@
     transport(1, whole, nothing, nothing)
     out_ref[...] = jnp.where(left((cols, lev)), land[0], land[1])
     for copy in sent:
-        copy.wait_send()
+        if id(copy) not in left_already:
+            copy.wait_send()
 
 
 def body(n_grp, n_tile, adjoint_in, departure, fraction, level_map, coarse_map):
@@ -404,7 +412,7 @@
             dma((2, max(2, n_grp - 1), CHUNKS)),
         ],
         compiler_params=pltpu.CompilerParams(
-            collective_id=0, has_side_effects=True, vmem_limit_bytes=48 * 2 ** 20
+            collective_id=0, has_side_effects=True, vmem_limit_bytes=60 * 2 ** 20
         ),
     )(adjoint_in, departure, fraction, level_map, coarse_map.transpose(1, 2, 0))
 

time: 71.3 us -> 68.8 us (0.965)
  local copies, waits for them, and re-layouts: 4.83 us -> 1.87 us
  Pallas kernels: 65.7 us -> 66.7 us
    unnamed x11 -> x1, local copies, waits for them, and re-layouts: 4.83 us -> 1.87 us
    pallas_call x1, Pallas kernels: 65.7 us -> 66.7 us  [body(): pl.pallas_call(functools.partial(kernel, n_grp, n_tile), out_shape=jax.Sh...]
where the time goes in v3:
time: 68.8 us; the launch traced here: 68.6 us
  Pallas kernels  66.7 us (97%)
  local copies, waits for them, and re-layouts  1.87 us (3%)
    pallas_call x1, Pallas kernels, body(): pl.pallas_call(functools.partial(kernel, n_grp, n_tile), out_shape=jax.Sh...  66.7 us
    unnamed x1, local copies, waits for them, and re-layouts  1.87 us

profile of v3, /device:TPU:1, one launch (start us, length us, event | category | flops | bytes accessed | tf_op | source)
XLA Modules:
  0.0 68.6 jit_solution(10727621606780940152)
XLA Ops:
  0.0 66.7 %shard_map.55 = f32[1024,128]{1,0:T(8,128)} custom-call(f32[1024,128]{1,0:T(8,128)} %x_hbm.1, s32[2,1024]{1,0:T(2,128)} %dep_hbm.1, f32[2,1024]{1,0:T(2,128)} %frac_hbm.1, f32[2,128,128]{2,1,0:T(8,128)} %lm_hbm.1, f32[4,4,128]{2,1,0:T(4,128)} %bitcast.1), custom_call_target="tpu_custom_call" | custom-call | tf_op jit(solution)/shard_map/pallas_call | solution.py:374
  66.8 1.9 %copy.7 = f32[1024,128]{1,0:T(8,128)} copy(f32[1024,128]{1,0:T(8,128)} %shard_map.55) | data formatting | bytes 1048576

commit v4 on v3

--- a/solution.py
+++ b/solution.py
@@ -42,7 +42,7 @@
 def kernel(
     n_grp, n_tile, x_hbm, dep_hbm, frac_hbm, lm_hbm, cm_hbm, out_ref,
     x_ref, dep_ref, frac_ref, lm_ref, cm_ref, meta_ref,
-    slots, pick, lifted, rows_out, rows_in, meta_out, meta_in, rows_hl,
+    slots, pick, meta_cols, lifted, rows_out, rows_in, meta_out, meta_in, rows_hl,
     s_high, s_low, land, edge, edge_in, field, grp_out, grp_in, grp_mid, grp_last,
     load_sem, rows_ss, rows_rs, meta_ss, meta_rs, edge_ss, edge_rs, grp_ss, grp_rs,
 ):
@@ -119,17 +119,23 @@
     def build_pick(t, j):
         @pl.loop(0, half // block)
         def _(i):
-            r = lax.broadcasted_iota(jnp.int32, (block, cols), 0) + i * block
-            hit = r == slots[8 * t + j : 8 * t + j + 1, :]
-            pick[t, j, pl.ds(pl.multiple_of(i * block, block), block), :] = jnp.where(hit, 1.0, 0.0).astype(BF16)
+            r = lax.broadcasted_iota(jnp.int32, (block, lane), 0) + i * block
+            at = pl.ds(pl.multiple_of(i * block, block), block)
+            for n in range(0, cols, lane):
+                hit = r == slots[8 * t + j : 8 * t + j + 1, n : n + lane]
+                pick[t, j, at, n : n + lane] = jnp.where(hit, 1.0, 0.0).astype(BF16)
+
+    def meta_columns(t):
+        whole = meta_ref[1 - t]
+        a = whole.astype(BF16).astype(F32)
+        parts = jnp.concatenate([a, whole - a, jnp.zeros((lane - 16, cols), F32)], axis=0)
+        meta_cols[t] = parts.T.astype(BF16)
 
     def do_meta(t, j):
-        whole = meta_ref[1 - t]
-        a = whole.astype(BF16)
-        rest = whole - a.astype(F32)
-        parts = jnp.concatenate([a.astype(F32), rest], axis=0).astype(BF16)
-        got = dot_nt(parts, pick[t, j])
-        packed = got[:8] + got[8:]
+        if j == 0:
+            meta_columns(t)
+        got = dot(pick[t, j], meta_cols[t]).T
+        packed = got[:8] + got[8:16]
         if j == REMOTE:
             meta_in[t, j] = packed
         else:
@@ -145,15 +151,16 @@
 
         @pl.loop(0, cols // size)
         def _(i):
-            cells = lax.broadcasted_iota(jnp.int32, (size, half), 0) + i * size
-            place = meta_in[t, j, 0:1, :].astype(jnp.int32)
-            value = jnp.zeros((size, half), F32)
-            for k in range(4):
-                value = jnp.where(cells == place + (k - 1), meta_in[t, j, 1 + k : 2 + k, :], value)
-            high, low = split(value)
+            cells = lax.broadcasted_iota(jnp.int32, (size, lane), 0) + i * size
             at = pl.ds(pl.multiple_of(i * size, size), size)
-            s_high[j, at, :] = high
-            s_low[j, at, :] = low
+            for n in range(0, half, lane):
+                place = meta_in[t, j, 0:1, n : n + lane].astype(jnp.int32)
+                value = jnp.zeros((size, lane), F32)
+                for k in range(4):
+                    value = jnp.where(cells == place + (k - 1), meta_in[t, j, 1 + k : 2 + k, n : n + lane], value)
+                high, low = split(value)
+                s_high[j, at, n : n + lane] = high
+                s_low[j, at, n : n + lane] = low
 
     part_lev = lev // 2
 
@@ -385,6 +392,7 @@
             pltpu.VMEM((2, 8, cols), F32),
             pltpu.VMEM((16, cols), jnp.int32),
             pltpu.VMEM((2, REMOTE + 1, half, cols), BF16),
+            pltpu.VMEM((2, cols, 128), BF16),
             pltpu.VMEM((cols, 2 * lev), BF16),
             pltpu.VMEM((2, 2, REMOTE, half // 2, lev), F32),
             pltpu.VMEM((2, 2, REMOTE + 1, half // 2, lev), F32),

time: 68.8 us -> 70.7 us (1.028)
  Pallas kernels: 66.7 us -> 68.6 us
    pallas_call x1, Pallas kernels: 66.7 us -> 68.6 us  [body(): pl.pallas_call(functools.partial(kernel, n_grp, n_tile), out_shape=jax.Sh...]
where the time goes in v4:
time: 70.7 us; the launch traced here: 70.5 us
  Pallas kernels  68.6 us (97%)
  local copies, waits for them, and re-layouts  1.87 us (3%)
    pallas_call x1, Pallas kernels, body(): pl.pallas_call(functools.partial(kernel, n_grp, n_tile), out_shape=jax.Sh...  68.6 us
    unnamed x1, local copies, waits for them, and re-layouts  1.87 us

profile of v4, /device:TPU:1, one launch (start us, length us, event | category | flops | bytes accessed | tf_op | source)
XLA Modules:
  0.0 70.5 jit_solution(16808051621960565439)
XLA Ops:
  0.0 68.6 %shard_map.55 = f32[1024,128]{1,0:T(8,128)} custom-call(f32[1024,128]{1,0:T(8,128)} %x_hbm.1, s32[2,1024]{1,0:T(2,128)} %dep_hbm.1, f32[2,1024]{1,0:T(2,128)} %frac_hbm.1, f32[2,128,128]{2,1,0:T(8,128)} %lm_hbm.1, f32[4,4,128]{2,1,0:T(4,128)} %bitcast.1), custom_call_target="tpu_custom_call" | custom-call | tf_op jit(solution)/shard_map/pallas_call | solution.py:381
  68.6 1.9 %copy.7 = f32[1024,128]{1,0:T(8,128)} copy(f32[1024,128]{1,0:T(8,128)} %shard_map.55) | data formatting | bytes 1048576

commit v5 on v4

--- a/solution.py
+++ b/solution.py
@@ -42,7 +42,7 @@
 def kernel(
     n_grp, n_tile, x_hbm, dep_hbm, frac_hbm, lm_hbm, cm_hbm, out_ref,
     x_ref, dep_ref, frac_ref, lm_ref, cm_ref, meta_ref,
-    slots, pick, meta_cols, lifted, rows_out, rows_in, meta_out, meta_in, rows_hl,
+    slots, pick, lifted, rows_out, rows_in, meta_out, meta_in, rows_hl,
     s_high, s_low, land, edge, edge_in, field, grp_out, grp_in, grp_mid, grp_last,
     load_sem, rows_ss, rows_rs, meta_ss, meta_rs, edge_ss, edge_rs, grp_ss, grp_rs,
 ):
@@ -125,17 +125,13 @@
                 hit = r == slots[8 * t + j : 8 * t + j + 1, n : n + lane]
                 pick[t, j, at, n : n + lane] = jnp.where(hit, 1.0, 0.0).astype(BF16)
 
-    def meta_columns(t):
+    def do_meta(t, j):
         whole = meta_ref[1 - t]
-        a = whole.astype(BF16).astype(F32)
-        parts = jnp.concatenate([a, whole - a, jnp.zeros((lane - 16, cols), F32)], axis=0)
-        meta_cols[t] = parts.T.astype(BF16)
-
-    def do_meta(t, j):
-        if j == 0:
-            meta_columns(t)
-        got = dot(pick[t, j], meta_cols[t]).T
-        packed = got[:8] + got[8:16]
+        a = whole.astype(BF16)
+        rest = whole - a.astype(F32)
+        parts = jnp.concatenate([a.astype(F32), rest], axis=0).astype(BF16)
+        got = dot_nt(parts, pick[t, j])
+        packed = got[:8] + got[8:]
         if j == REMOTE:
             meta_in[t, j] = packed
         else:
@@ -392,7 +388,6 @@
             pltpu.VMEM((2, 8, cols), F32),
             pltpu.VMEM((16, cols), jnp.int32),
             pltpu.VMEM((2, REMOTE + 1, half, cols), BF16),
-            pltpu.VMEM((2, cols, 128), BF16),
             pltpu.VMEM((cols, 2 * lev), BF16),
             pltpu.VMEM((2, 2, REMOTE, half // 2, lev), F32),
             pltpu.VMEM((2, 2, REMOTE + 1, half // 2, lev), F32),

time: 70.7 us -> 69.1 us (0.977)
  Pallas kernels: 68.6 us -> 67.1 us
    pallas_call x1, Pallas kernels: 68.6 us -> 67.1 us  [body(): pl.pallas_call(functools.partial(kernel, n_grp, n_tile), out_shape=jax.Sh...]
where the time goes in v5:
time: 69.1 us; the launch traced here: 68.9 us
  Pallas kernels  67.1 us (97%)
  local copies, waits for them, and re-layouts  1.87 us (3%)
    pallas_call x1, Pallas kernels, body(): pl.pallas_call(functools.partial(kernel, n_grp, n_tile), out_shape=jax.Sh...  67.1 us
    unnamed x1, local copies, waits for them, and re-layouts  1.87 us

profile of v5, /device:TPU:1, one launch (start us, length us, event | category | flops | bytes accessed | tf_op | source)
XLA Modules:
  0.0 68.9 jit_solution(10311998252385409280)
XLA Ops:
  0.0 67.1 %shard_map.55 = f32[1024,128]{1,0:T(8,128)} custom-call(f32[1024,128]{1,0:T(8,128)} %x_hbm.1, s32[2,1024]{1,0:T(2,128)} %dep_hbm.1, f32[2,1024]{1,0:T(2,128)} %frac_hbm.1, f32[2,128,128]{2,1,0:T(8,128)} %lm_hbm.1, f32[4,4,128]{2,1,0:T(4,128)} %bitcast.1), custom_call_target="tpu_custom_call" | custom-call | tf_op jit(solution)/shard_map/pallas_call | solution.py:377
  67.1 1.9 %copy.7 = f32[1024,128]{1,0:T(8,128)} copy(f32[1024,128]{1,0:T(8,128)} %shard_map.55) | data formatting | bytes 1048576

commit v6 on v3

--- a/solution.py
+++ b/solution.py
@@ -262,13 +262,12 @@
             build_spread(t, REMOTE)
         for q in range(2):
             deposit(t, q, REMOTE, True)
-        if t == 0:
-            for j in range(REMOTE):
-                build_spread(t, j)
         for j in (2, 3, 0, 1):
             copies[0][j].wait_send()
             left_already.append(id(copies[0][j]))
             send_rows(1, j)
+            if t == 0:
+                build_spread(t, j)
         for q in range(2):
             for j in ARRIVE:
                 copies[q][j].wait_recv()

time: 68.8 us -> 71 us (1.032)
  Pallas kernels: 66.7 us -> 68.9 us
    pallas_call x1, Pallas kernels: 66.7 us -> 68.9 us  [body(): pl.pallas_call(functools.partial(kernel, n_grp, n_tile), out_shape=jax.Sh...]
where the time goes in v6:
time: 71 us; the launch traced here: 70.8 us
  Pallas kernels  68.9 us (97%)
  local copies, waits for them, and re-layouts  1.87 us (3%)
    pallas_call x1, Pallas kernels, body(): pl.pallas_call(functools.partial(kernel, n_grp, n_tile), out_shape=jax.Sh...  68.9 us
    unnamed x1, local copies, waits for them, and re-layouts  1.87 us

profile of v6, /device:TPU:1, one launch (start us, length us, event | category | flops | bytes accessed | tf_op | source)
XLA Modules:
  0.0 70.8 jit_solution(2980262009576111540)
XLA Ops:
  0.0 68.9 %shard_map.55 = f32[1024,128]{1,0:T(8,128)} custom-call(f32[1024,128]{1,0:T(8,128)} %x_hbm.1, s32[2,1024]{1,0:T(2,128)} %dep_hbm.1, f32[2,1024]{1,0:T(2,128)} %frac_hbm.1, f32[2,128,128]{2,1,0:T(8,128)} %lm_hbm.1, f32[4,4,128]{2,1,0:T(4,128)} %bitcast.1), custom_call_target="tpu_custom_call" | custom-call | tf_op jit(solution)/shard_map/pallas_call | solution.py:373
  68.9 1.9 %copy.7 = f32[1024,128]{1,0:T(8,128)} copy(f32[1024,128]{1,0:T(8,128)} %shard_map.55) | data formatting | bytes 1048576
